TPU v7x, 32 devices: a whole 2x2x4 slice. The times are simulated.
32 devices in a mesh: view: 8 (over z, y), brick: 4 (over x, core).
Axes of the slice: x: 2, y: 2, z: 4, core: 2. Of those that a mesh axis runs over, the one named last changes fastest.
Arguments:
- volume: float32 [8, 8, 32, 128], P('brick'), may hold values from -6 to 6
- offsets: float32 [8, 3], P('view'), may hold values from 0 to 1
- shifts: int32 [8, 2], P('view'), may hold values from 0 to 127
- order: int32 [8], P('view'), may hold values from 0 to 1
- cond: float32 [8, 8], P('view'), may hold values from -6 to 6
- w_in: float32 [16, 128], replicated, may hold values from -1.5 to 1.5
- w_mid: float32 [128, 128], replicated, may hold values from -0.5 to 0.5
- w_out: float32 [128, 4], replicated, may hold values from -0.5 to 0.5
- cot_image: float32 [8, 3, 32, 128], P('view', None, 'brick'), may hold values from -0.12 to 0.12
Outputs:
- image: float32 [8, 3, 32, 128], P('view', None, 'brick')
- grad_in: float32 [16, 128], replicated
- grad_mid: float32 [128, 128], replicated
- grad_out: float32 [128, 4], replicated
Inputs may be any that keep to these rules, and one draw needn't show every extreme that they name: `order`: 0 marches towards higher slice numbers, 1 towards lower ones.
All inputs are finite; a program needn't handle non-finite values.
Results may differ from a plain program's by a relative error of at most 0.0003.
Values sent between devices are 32-bit elements; how exact they have to be, the bound alone decides.
A program may use at most 64 MiB of HBM per device.

v0:
```python
import functools

import jax
import jax.numpy as jnp
from jax import lax
from jax.experimental import pallas as pl
from jax.experimental.pallas import tpu as pltpu
from jax.sharding import PartitionSpec as P

STEP_DEPTH = 0.15
MESH = pl.DeviceIdType.MESH
F32 = jnp.float32
BF16 = jnp.bfloat16
TILE = 8


def split(x):
    high = x.astype(BF16)
    return high, (x - high.astype(F32)).astype(BF16)


def dot(a, b):
    return lax.dot_general(a, b, (((1,), (0,)), ((), ())), preferred_element_type=F32)


def stacked(high, low):
    return jnp.concatenate([jnp.concatenate([high, high], 1), jnp.concatenate([low, low], 1)], 0)


def dot_stacked(a, b):
    out = dot(a, b)
    rows = out.shape[0] // 2
    return out[:rows] + out[rows:]


def blocks(a, b):
    out = lax.dot_general(a, b, (((1,), (1,)), ((), ())), preferred_element_type=F32)
    rows, cols = out.shape[0] // 2, out.shape[1] // 2
    return (out[rows:, cols:] + out[rows:, :cols] + out[:rows, cols:]) + out[:rows, :cols]


def activate(u):
    gate = 0.5 * jnp.tanh(0.5 * u) + 0.5
    h = u * gate
    return h, gate + h * (1.0 - gate)


def one_minus_exp(x):
    series = x * (1.0 - x * (1 / 2) * (1.0 - x * (1 / 3) * (1.0 - x * (1 / 4) * (1.0 - x * (1 / 5)))))
    e = jnp.exp(-x)
    return jnp.where(x < 0.0625, series, 1.0 - e), e


def kernel(
    views, bricks, S, R, C, RC, RB, hid,
    vol, offsets, shifts, order, cond, w_in, w_mid, w_out, cot,
    image, final_out,
    halo, shifted, feats, h1, d1, h2, d2, emit, gate, part, cots,
    wi_s, wm_s, wo_s, wmb_s, wob_s, grads, landed, final,
    halo_sems, cot_send, cot_recv, part_send, part_recv, tile_send, tile_recv, last_send, last_recv,
):
    CH = 8
    N = views * bricks
    T = grads.shape[0]
    nch = R // RC
    n = RC * C
    v = lax.axis_index("view")
    b = lax.axis_index("brick")
    me = v * bricks + b

    def place(k):
        return (k // bricks, k % bricks)

    barrier = pltpu.get_barrier_semaphore()

    @pl.loop(1, N)
    def _(k):
        pl.semaphore_signal(barrier, inc=1, device_id=place((me + k) % N), device_id_type=MESH)

    f0, f1, f2 = offsets[0, 0], offsets[0, 1], offsets[0, 2]
    s0 = lax.rem(shifts[0, 0], R)
    s1 = lax.rem(shifts[0, 1], C)
    back = order[0] == 1

    for i in range(RB):
        cots[b * RB + i, pl.ds(0, 1), :] = jnp.zeros((1, C), F32)
        for c in range(3):
            cots[b * RB + i, pl.ds(1 + c, 1), :] = cot[0, c, pl.ds(i, 1), :]

    wi_hi, wi_lo = split(w_in[...].T)
    wi_s[...] = jnp.concatenate([wi_hi.astype(F32), wi_hi.astype(F32), wi_lo.astype(F32)], 1).astype(BF16)
    wm_hi, wm_lo = split(w_mid[...].T)
    wm_s[...] = stacked(wm_hi, wm_lo)
    wmb_hi, wmb_lo = split(w_mid[...])
    wmb_s[...] = stacked(wmb_hi, wmb_lo)
    wo_t = jnp.concatenate([w_out[...], jnp.zeros_like(w_out)], 0)
    wo_hi = wo_t.astype(BF16).astype(F32)
    wo_lo = wo_t - wo_hi
    wo_s[...] = stacked(wo_hi, wo_lo).astype(BF16)
    wob_s[...] = jnp.concatenate([wo_hi, wo_hi, wo_lo, jnp.zeros_like(wo_lo)], 0).T.astype(BF16)

    def resample(s):
        for i in range(R):
            near = vol[s, pl.ds(i, CH, stride=R), :]
            far = vol[s + 1, pl.ds(i, CH, stride=R), :] if s + 1 < S else halo[pl.ds(i, CH, stride=R), :]
            deep = (1.0 - f2) * near + f2 * far
            first = pltpu.roll(deep, lax.rem(C - s1, C), 1)
            second = pltpu.roll(deep, lax.rem(2 * C - 1 - s1, C), 1)
            mixed = (1.0 - f1) * first + f1 * second
            shifted[s, i] = mixed
            shifted[s, R + i] = mixed
            if i == 0:
                shifted[s, 2 * R] = mixed

    row = lax.broadcasted_iota(jnp.int32, (CH, n), 0)
    cond_rows = jnp.zeros((CH, n), F32)
    for c in range(CH):
        cond_rows = jnp.where(row == c, cond[0, c], cond_rows)
    chan = lax.broadcasted_iota(jnp.int32, (RC, 4, C), 1)

    def forward(s, c):
        rows = shifted[s, pl.ds(s0 + c * RC, RC + 1)]
        mixed = (1.0 - f0) * rows[:-1] + f0 * rows[1:]
        feat = jnp.concatenate([jnp.concatenate([mixed[i] for i in range(RC)], 1), cond_rows], 0)
        hi, lo = split(feat)
        feats[s, c] = jnp.concatenate([hi, lo], 0)
        h, d = activate(dot(wi_s[...], jnp.concatenate([hi, lo, hi], 0)))
        d1[s, c] = d
        both = jnp.concatenate(split(h), 0)
        h1[s, c] = both
        h, d = activate(dot_stacked(wm_s[...], both))
        d2[s, c] = d
        both = jnp.concatenate(split(h), 0)
        h2[s, c] = both
        raw = dot_stacked(wo_s[...], both)
        x = jnp.stack([raw[:4, i * C:(i + 1) * C] for i in range(RC)], 0)
        e = jnp.exp(-jnp.abs(x))
        r = 1.0 / (1.0 + e)
        sg = jnp.where(x >= 0, r, e * r)
        log1p = jnp.where(
            e < 0.0625, e * (1.0 - e * (1 / 2 - e * (1 / 3 - e * (1 / 4 - e * (1 / 5 - e * (1 / 6)))))), jnp.log(1.0 + e)
        )
        sp = jnp.maximum(x, 0.0) + log1p
        gate[s, pl.ds(c * RC, RC)] = sg
        emit[s, pl.ds(c * RC, RC)] = jnp.where(chan == 0, STEP_DEPTH * sp, sg)

    def marched(ref, rows, m):
        return jnp.where(back, ref[S - 1 - m, rows], ref[m, rows])

    def part_copy(c, k, brick):
        rows = pl.ds(c * RC, RC)
        return pltpu.make_async_remote_copy(
            src_ref=part.at[brick, rows], dst_ref=part.at[brick, rows],
            send_sem=part_send.at[c, k], recv_sem=part_recv.at[c, k],
            device_id=(v, (b + k) % bricks), device_id_type=MESH,
        )

    def composite(c):
        rows = pl.ds(c * RC, RC)
        transmit = jnp.ones((RC, 1, C), F32)
        colour = jnp.zeros((RC, 4, C), F32)
        for m in range(S):
            em = marched(emit, rows, m)
            opacity, e = one_minus_exp(em[:, 0:1, :])
            colour = colour + (transmit * opacity) * em
            transmit = transmit * e
        part[b, rows] = jnp.where(chan == 0, transmit, colour)

    def cot_copy(k, brick):
        rows = pl.ds(brick * RB, RB)
        return pltpu.make_async_remote_copy(
            src_ref=cots.at[rows], dst_ref=cots.at[rows],
            send_sem=cot_send.at[k], recv_sem=cot_recv.at[k],
            device_id=(v, (b + k) % bricks), device_id_type=MESH,
        )

    def halo_copy():
        return pltpu.make_async_remote_copy(
            src_ref=vol.at[0], dst_ref=halo, send_sem=halo_sems.at[0], recv_sem=halo_sems.at[1],
            device_id=(v, (b + bricks - 1) % bricks), device_id_type=MESH,
        )

    for s in range(S - 1):
        resample(s)

    ahead = nch // 2
    for s in range(S - 1):
        @pl.loop(0, ahead)
        def _(c, s=s):
            forward(s, c)

    pl.semaphore_wait(barrier, N - 1)

    @pl.when(b > 0)
    def _():
        halo_copy().start()

    for k in range(1, bricks):
        cot_copy(k, b).start()

    for s in range(S - 1):
        @pl.loop(ahead, nch)
        def _(c, s=s):
            forward(s, c)

    @pl.when(b == bricks - 1)
    def _():
        halo[...] = jnp.zeros_like(halo)

    @pl.when(b < bricks - 1)
    def _():
        halo_copy().wait_recv()

    resample(S - 1)

    @pl.loop(0, nch)
    def _(c):
        forward(S - 1, c)
        composite(c)
        for k in range(1, bricks):
            part_copy(c, k, b).start()

    for k in range(1, bricks):
        cot_copy(k, (b + bricks - k) % bricks).wait_recv()
    grads[...] = jnp.zeros_like(grads)
    position = jnp.where(back, bricks - 1 - b, b)

    def ordered(rows, p):
        return jnp.where(back, part[bricks - 1 - p, rows], part[p, rows])

    @pl.loop(0, nch)
    def _(c):
        rows = pl.ds(c * RC, RC)
        for k in range(1, bricks):
            part_copy(c, k, (b + bricks - k) % bricks).wait_recv()
        front = jnp.ones((RC, 1, C), F32)
        behind = jnp.zeros((RC, 4, C), F32)
        for p in range(bricks - 1):
            front = jnp.where(p < position, front * ordered(rows, p)[:, 0:1, :], front)
        for p in reversed(range(1, bricks)):
            here = ordered(rows, p)
            behind = jnp.where(p > position, here + here[:, 0:1, :] * behind, behind)
        grad = cots[rows] * front
        behind = jnp.sum(jnp.where(chan == 0, 0.0, grad * behind), 1, keepdims=True)
        transmit = jnp.ones((RC, 1, C), F32)
        steps = []
        for m in range(S):
            em = marched(emit, rows, m)
            opacity, e = one_minus_exp(em[:, 0:1, :])
            steps.append((em, marched(gate, rows, m), transmit * opacity, transmit * e))
            transmit = transmit * e
        tail = behind * transmit
        draws = [None] * S
        for m in reversed(range(S)):
            em, sg, weight, later = steps[m]
            q = jnp.sum(jnp.where(chan == 0, 0.0, grad * em), 1, keepdims=True)
            d_optical = q * later - tail
            tail = tail + q * weight
            draws[m] = jnp.where(chan == 0, d_optical * STEP_DEPTH * sg, grad * weight * (sg * (1.0 - sg)))
        for s in range(S):
            draw = jnp.where(back, draws[S - 1 - s], draws[s])
            draw = jnp.concatenate([draw[i] for i in range(RC)], 1)
            draw = jnp.concatenate([draw, jnp.zeros_like(draw)], 0)
            high = draw.astype(BF16).astype(F32)
            low = draw - high
            d_raw = jnp.concatenate([high, low, high, jnp.zeros_like(high)], 0).astype(BF16)
            g_out = blocks(d_raw[:2 * TILE], h2[s, c])
            du2 = dot(wob_s[...], d_raw) * d2[s, c]
            both = jnp.concatenate(split(du2), 0)
            g_mid = blocks(h1[s, c], both)
            du1 = dot_stacked(wmb_s[...], both) * d1[s, c]
            g_in = blocks(feats[s, c], jnp.concatenate(split(du1), 0))
            grads[0:2] += g_in.reshape(2, TILE, hid)
            grads[2:T - 1] += g_mid.reshape(T - 3, TILE, hid)
            grads[T - 1] += g_out

    def owner(t):
        return (t * N) // T

    def tile_copy(t, slot):
        return pltpu.make_async_remote_copy(
            src_ref=grads.at[t], dst_ref=landed.at[slot],
            send_sem=tile_send.at[t], recv_sem=tile_recv.at[slot],
            device_id=place(owner(t)), device_id_type=MESH,
        )

    def last_copy(t, k):
        return pltpu.make_async_remote_copy(
            src_ref=final.at[t], dst_ref=final.at[t],
            send_sem=last_send.at[k], recv_sem=last_recv.at[t],
            device_id=place((me + k) % N), device_id_type=MESH,
        )

    @pl.loop(0, T)
    def _(t):
        @pl.when(owner(t) != me)
        def _():
            tile_copy(t, (me - owner(t) + N - 1) % N).start()

    own = pl.ds(b * RB, RB)
    transmit = jnp.ones((RB, 1, C), F32)
    colour = jnp.zeros((RB, 4, C), F32)
    for p in range(bricks):
        here = ordered(own, p)
        colour = colour + transmit * here
        transmit = transmit * here[:, 0:1, :]
    for i in range(RB):
        for c in range(3):
            image[0, c, pl.ds(i, 1), :] = colour[i, 1 + c:2 + c, :]

    my_tile = (me * T + N - 1) // N
    owns = owner(my_tile) == me

    @pl.when(owns)
    def _():
        @pl.loop(0, N - 1)
        def _(k):
            tile_copy(my_tile, k).wait_recv()

        final[my_tile] = grads[my_tile] + jnp.sum(landed[...], 0)

        @pl.loop(1, N)
        def _(k):
            last_copy(my_tile, k).start()

    @pl.when(b > 0)
    def _():
        halo_copy().wait_send()

    for k in range(1, bricks):
        cot_copy(k, b).wait_send()

    @pl.loop(0, nch)
    def _(c):
        for k in range(1, bricks):
            part_copy(c, k, b).wait_send()

    @pl.loop(0, T)
    def _(t):
        @pl.when(owner(t) != me)
        def _():
            tile_copy(t, 0).wait_send()
            last_copy(t, 1).wait_recv()

    final_out[...] = final[...]

    @pl.when(owns)
    def _():
        @pl.loop(1, N)
        def _(k):
            last_copy(my_tile, k).wait_send()


def deliver(picture, tiles, image, out_in, out_mid, out_out):
    T, _, hid = tiles.shape
    image[...] = picture[...]
    out_in[...] = tiles[0:2].reshape(2 * TILE, hid)
    out_mid[...] = tiles[2:T - 1].reshape(hid, hid)
    out_out[...] = tiles[T - 1][:4]


def per_device(volume, offsets, shifts, order, cond, w_in, w_mid, w_out, cot_image):
    views, bricks = lax.axis_size("view"), lax.axis_size("brick")
    N = views * bricks
    S, CH, R, C = volume.shape
    RB = cot_image.shape[2]
    fin, hid = w_in.shape
    RC = min(8, R)
    nch = R // RC
    n = RC * C
    T = (fin + hid) // TILE + 1
    vmem = pl.BlockSpec(memory_space=pltpu.VMEM)
    smem = pl.BlockSpec(memory_space=pltpu.SMEM)
    kept = lambda rows, kind: pltpu.VMEM((S, nch, rows, n), kind)
    dma = lambda *shape: pltpu.SemaphoreType.DMA(shape)
    image, tiles = pl.pallas_call(
        functools.partial(kernel, views, bricks, S, R, C, RC, RB, hid),
        out_shape=(
            jax.ShapeDtypeStruct((1, 3, RB, C), F32),
            jax.ShapeDtypeStruct((T, TILE, hid), F32),
        ),
        in_specs=[vmem, smem, smem, smem, smem, vmem, vmem, vmem, vmem],
        out_specs=(vmem, vmem),
        scratch_shapes=[
            pltpu.VMEM((CH * R, C), F32),
            pltpu.VMEM((S, 2 * R + 1, CH, C), F32),
            kept(2 * fin, BF16), kept(2 * hid, BF16), kept(hid, F32), kept(2 * hid, BF16), kept(hid, F32),
            pltpu.VMEM((S, R, 4, C), F32),
            pltpu.VMEM((S, R, 4, C), F32),
            pltpu.VMEM((bricks, R, 4, C), F32),
            pltpu.VMEM((R, 4, C), F32),
            pltpu.VMEM((hid, 3 * fin), BF16),
            pltpu.VMEM((2 * hid, 2 * hid), BF16),
            pltpu.VMEM((2 * TILE, 2 * hid), BF16),
            pltpu.VMEM((2 * hid, 2 * hid), BF16),
            pltpu.VMEM((hid, 4 * TILE), BF16),
            pltpu.VMEM((T, TILE, hid), F32),
            pltpu.VMEM((N - 1, TILE, hid), F32),
            pltpu.VMEM((T, TILE, hid), F32),
            dma(2), dma(bricks), dma(bricks), dma(nch, bricks), dma(nch, bricks),
            dma(T), dma(N - 1), dma(N), dma(T),
        ],
        compiler_params=pltpu.CompilerParams(
            collective_id=0, has_side_effects=True, vmem_limit_bytes=40 * 1024 * 1024
        ),
        cost_estimate=pl.CostEstimate(
            flops=2 * S * R * C * hid * (3 * hid + 3 * fin + 12), bytes_accessed=4 * volume.size,
            transcendentals=2 * S * R * C * hid,
        ),
    )(volume.reshape(S, CH * R, C), offsets, shifts, order, cond, w_in, w_mid, w_out.T, cot_image)
    image, g_in, g_mid, g_out = pl.pallas_call(
        deliver,
        out_shape=(
            jax.ShapeDtypeStruct((1, 3, RB, C), F32),
            jax.ShapeDtypeStruct((fin, hid), F32),
            jax.ShapeDtypeStruct((hid, hid), F32),
            jax.ShapeDtypeStruct((4, hid), F32),
        ),
        in_specs=[vmem, vmem],
        out_specs=(vmem, vmem, vmem, vmem),
        compiler_params=pltpu.CompilerParams(vmem_limit_bytes=4 * 1024 * 1024),
    )(image, tiles)
    return image, g_in, g_mid, g_out.T


def solution(mesh):
    placed = (
        P("brick", None, None, None),
        P("view", None),
        P("view", None),
        P("view"),
        P("view", None),
        P(),
        P(),
        P(),
        P("view", None, "brick", None),
    )
    return jax.shard_map(
        per_device,
        mesh=mesh,
        in_specs=placed,
        out_specs=(P("view", None, "brick", None), P(), P(), P()),
        check_vma=False,
    )
```

profile of v0, /device:TPU:0, one launch (start us, length us, event | category | flops | bytes accessed | tf_op | source)
XLA Modules:
  0.0 38.0 jit_solution(8304176853689341954)
XLA Ops:
  1.3 0.0 copy-start.4
  1.3 0.0 copy-start.5
  1.3 0.0 copy-start.6
  1.3 0.0 copy-start.7
  1.3 0.6 %copy-done.4 = f32[128,4]{0,1:T(4,128)S(1)} copy-done((f32[128,4]{0,1:T(4,128)S(1)}, f32[128,4]{0,1:T(4,128)}, u32[]{:S(2)}) %copy-start.4) | copy-done | bytes 2072
  2.0 0.0 copy-done.5
  2.0 0.0 copy-done.6
  2.0 0.0 copy-done.7
  2.0 0.0 copy-start
  2.0 0.9 %copy-done = f32[2,8,32,128]{3,2,1,0:T(8,128)S(1)} copy-done((f32[2,8,32,128]{3,2,1,0:T(8,128)S(1)}, f32[2,8,32,128]{3,2,1,0:T(8,128)}, u32[]{:S(2)}) %copy-start) | copy-done | bytes 262168
  2.9 0.0 copy-start.1
  2.9 0.8 %copy-done.1 = f32[128,128]{1,0:T(8,128)S(1)} copy-done((f32[128,128]{1,0:T(8,128)S(1)}, f32[128,128]{1,0:T(8,128)}, u32[]{:S(2)}) %copy-start.1) | copy-done | bytes 65560
  3.8 0.0 copy-start.2
  3.8 0.7 %copy-done.2 = f32[1,3,8,128]{3,2,1,0:T(8,128)S(1)} copy-done((f32[1,3,8,128]{3,2,1,0:T(8,128)S(1)}, f32[1,3,8,128]{3,2,1,0:T(8,128)}, u32[]{:S(2)}) %copy-start.2) | copy-done | bytes 12312
  4.5 0.0 copy-start.3
  4.5 0.7 %copy-done.3 = f32[16,128]{1,0:T(8,128)S(1)} copy-done((f32[16,128]{1,0:T(8,128)S(1)}, f32[16,128]{1,0:T(8,128)}, u32[]{:S(2)}) %copy-start.3) | copy-done | bytes 8216
  5.2 32.2 %shard_map.120 = (f32[1,3,8,128]{3,2,1,0:T(8,128)S(1)}, f32[19,8,128]{2,1,0:T(8,128)S(1)}) custom-call(f32[2,256,128]{2,1,0:T(8,128)S(1)} %bitcast.3, f32[1,3]{1,0:T(1,128)S(1)} %copy-done.5, s32[1,2]{1,0:T(1,128)S(1)} %copy-done.6, s32[1]{0:T(128)S(6)} %copy.13.order, f32[1,8]{1,0:T(1,128)S(1)} %copy-done.7, f32[16,128]{1,0:T(8,128)S(1)} %copy-done.3, ...), custom_call_target="tpu_custom_call" | custom-call | flops 931135488 | bytes 262144 | tf_op jit(solution)/shard_map/pallas_call | solution.py:376
  37.3 0.6 %shard_map.121 = (f32[1,3,8,128]{3,2,1,0:T(8,128)}, f32[16,128]{1,0:T(8,128)}, f32[128,128]{1,0:T(8,128)}, f32[4,128]{1,0:T(4,128)}) custom-call(f32[1,3,8,128]{3,2,1,0:T(8,128)S(1)} %get-tuple-element.10.picture, f32[19,8,128]{2,1,0:T(8,128)S(1)} %get-tuple-element.11.tiles), custom_call_target="tpu_custom_call" | custom-call | tf_op jit(solution)/shard_map/pallas_call | solution.py:411
Async XLA Ops:
  1.3 0.7 %copy-start.4 = (f32[128,4]{0,1:T(4,128)S(1)}, f32[128,4]{0,1:T(4,128)}, u32[]{:S(2)}) copy-start(f32[128,4]{0,1:T(4,128)} %param.16) | copy-start | bytes 6148
  1.3 0.7 %copy-start.5 = (f32[1,3]{1,0:T(1,128)S(1)}, f32[1,3]{1,0:T(1,128)}, u32[]{:S(2)}) copy-start(f32[1,3]{1,0:T(1,128)} %offsets.1) | copy-start | bytes 40
  1.3 0.7 %copy-start.6 = (s32[1,2]{1,0:T(1,128)S(1)}, s32[1,2]{1,0:T(1,128)}, u32[]{:S(2)}) copy-start(s32[1,2]{1,0:T(1,128)} %shifts.1) | copy-start | bytes 28
  1.3 0.7 %copy-start.7 = (f32[1,8]{1,0:T(1,128)S(1)}, f32[1,8]{1,0:T(1,128)}, u32[]{:S(2)}) copy-start(f32[1,8]{1,0:T(1,128)} %cond.1) | copy-start | bytes 100
  2.0 0.9 %copy-start = (f32[2,8,32,128]{3,2,1,0:T(8,128)S(1)}, f32[2,8,32,128]{3,2,1,0:T(8,128)}, u32[]{:S(2)}) copy-start(f32[2,8,32,128]{3,2,1,0:T(8,128)} %param.9) | copy-start | bytes 786436
  2.9 0.8 %copy-start.1 = (f32[128,128]{1,0:T(8,128)S(1)}, f32[128,128]{1,0:T(8,128)}, u32[]{:S(2)}) copy-start(f32[128,128]{1,0:T(8,128)} %w_mid.1) | copy-start | bytes 196612
  3.8 0.7 %copy-start.2 = (f32[1,3,8,128]{3,2,1,0:T(8,128)S(1)}, f32[1,3,8,128]{3,2,1,0:T(8,128)}, u32[]{:S(2)}) copy-start(f32[1,3,8,128]{3,2,1,0:T(8,128)} %cot.1) | copy-start | bytes 36868
  4.5 0.7 %copy-start.3 = (f32[16,128]{1,0:T(8,128)S(1)}, f32[16,128]{1,0:T(8,128)}, u32[]{:S(2)}) copy-start(f32[16,128]{1,0:T(8,128)} %w_in.1) | copy-start | bytes 24580
where the time goes:
time: 38.3 us; the launch traced here: 38 us
  Pallas kernels  32.8 us (86%)
  local copies, waits for them, and re-layouts  3.86 us (10%)
  between operations  1.32 us (3%)
    pallas_call x1, Pallas kernels, per_device(): pl.pallas_call(functools.partial(kernel, views, bricks, S, R, C, RC, RB,...  32.2 us
    unnamed x16, local copies, waits for them, and re-layouts  3.86 us

commit v1 on v0

--- a/solution.py
+++ b/solution.py
@@ -39,6 +39,14 @@
     return (out[rows:, cols:] + out[rows:, :cols] + out[:rows, cols:]) + out[:rows, :cols]
 
 
+def staggered(parts):
+    waiting, active = list(parts), []
+    while waiting or active:
+        if waiting:
+            active.append(waiting.pop(0))
+        active = [part for part in active if next(part, part) is not part]
+
+
 def activate(u):
     gate = 0.5 * jnp.tanh(0.5 * u) + 0.5
     h = u * gate
@@ -53,9 +61,10 @@
 
 def kernel(
     views, bricks, S, R, C, RC, RB, hid,
-    vol, offsets, shifts, order, cond, w_in, w_mid, w_out, cot,
+    vol_far, offsets, shifts, order, cond, w_in_far, w_mid_far, w_out_far, cot_far,
     image, final_out,
-    halo, shifted, feats, h1, d1, h2, d2, emit, gate, part, cots,
+    vol, w_in, w_mid, w_out, cot, in_sems,
+    halo, shifted, feats, h1, d1, h2, d2, du2s, du1s, emit, gate, part, cots,
     wi_s, wm_s, wo_s, wmb_s, wob_s, grads, landed, final,
     halo_sems, cot_send, cot_recv, part_send, part_recv, tile_send, tile_recv, last_send, last_recv,
 ):
@@ -64,12 +73,22 @@
     T = grads.shape[0]
     nch = R // RC
     n = RC * C
+    SUB = min(2 * C, n)
     v = lax.axis_index("view")
     b = lax.axis_index("brick")
     me = v * bricks + b
 
     def place(k):
         return (k // bricks, k % bricks)
+
+    arrive = [
+        pltpu.make_async_copy(far, near, in_sems.at[i])
+        for i, (far, near) in enumerate(
+            ((vol_far, vol), (w_in_far, w_in), (w_mid_far, w_mid), (w_out_far, w_out), (cot_far, cot))
+        )
+    ]
+    for copy in arrive:
+        copy.start()
 
     barrier = pltpu.get_barrier_semaphore()
 
@@ -81,6 +100,9 @@
     s0 = lax.rem(shifts[0, 0], R)
     s1 = lax.rem(shifts[0, 1], C)
     back = order[0] == 1
+
+    for copy in arrive:
+        copy.wait()
 
     for i in range(RB):
         cots[b * RB + i, pl.ds(0, 1), :] = jnp.zeros((1, C), F32)
@@ -112,27 +134,37 @@
             if i == 0:
                 shifted[s, 2 * R] = mixed
 
-    row = lax.broadcasted_iota(jnp.int32, (CH, n), 0)
-    cond_rows = jnp.zeros((CH, n), F32)
+    row = lax.broadcasted_iota(jnp.int32, (CH, SUB), 0)
+    cond_rows = jnp.zeros((CH, SUB), F32)
     for c in range(CH):
         cond_rows = jnp.where(row == c, cond[0, c], cond_rows)
     chan = lax.broadcasted_iota(jnp.int32, (RC, 4, C), 1)
 
+    def forward_part(s, c, j, mixed, raws):
+        here = (s, c, slice(None), pl.ds(j * SUB, SUB))
+        rows = range(j * SUB // C, (j + 1) * SUB // C)
+        feat = jnp.concatenate([jnp.concatenate([mixed[i] for i in rows], 1), cond_rows], 0)
+        hi, lo = split(feat)
+        feats[here] = jnp.concatenate([hi, lo], 0)
+        u = dot(wi_s[...], jnp.concatenate([hi, lo, hi], 0))
+        yield
+        h, d1[here] = activate(u)
+        both = jnp.concatenate(split(h), 0)
+        h1[here] = both
+        u = dot_stacked(wm_s[...], both)
+        yield
+        h, d2[here] = activate(u)
+        both = jnp.concatenate(split(h), 0)
+        h2[here] = both
+        raws[j] = dot_stacked(wo_s[...], both)
+        yield
+
     def forward(s, c):
         rows = shifted[s, pl.ds(s0 + c * RC, RC + 1)]
         mixed = (1.0 - f0) * rows[:-1] + f0 * rows[1:]
-        feat = jnp.concatenate([jnp.concatenate([mixed[i] for i in range(RC)], 1), cond_rows], 0)
-        hi, lo = split(feat)
-        feats[s, c] = jnp.concatenate([hi, lo], 0)
-        h, d = activate(dot(wi_s[...], jnp.concatenate([hi, lo, hi], 0)))
-        d1[s, c] = d
-        both = jnp.concatenate(split(h), 0)
-        h1[s, c] = both
-        h, d = activate(dot_stacked(wm_s[...], both))
-        d2[s, c] = d
-        both = jnp.concatenate(split(h), 0)
-        h2[s, c] = both
-        raw = dot_stacked(wo_s[...], both)
+        raws = [None] * (n // SUB)
+        staggered([forward_part(s, c, j, mixed, raws) for j in range(n // SUB)])
+        raw = jnp.concatenate(raws, 1)
         x = jnp.stack([raw[:4, i * C:(i + 1) * C] for i in range(RC)], 0)
         e = jnp.exp(-jnp.abs(x))
         r = 1.0 / (1.0 + e)
@@ -227,6 +259,17 @@
 
     def ordered(rows, p):
         return jnp.where(back, part[bricks - 1 - p, rows], part[p, rows])
+
+    def backward_part(s, c, j, d_raw):
+        lanes = pl.ds(j * SUB, SUB)
+        u = dot(wob_s[...], d_raw[:, j * SUB:(j + 1) * SUB])
+        yield
+        both = jnp.concatenate(split(u * d2[s, c, :, lanes]), 0)
+        du2s[s, :, lanes] = both
+        u = dot_stacked(wmb_s[...], both)
+        yield
+        du1s[s, :, lanes] = jnp.concatenate(split(u * d1[s, c, :, lanes]), 0)
+        yield
 
     @pl.loop(0, nch)
     def _(c):
@@ -257,6 +300,7 @@
             d_optical = q * later - tail
             tail = tail + q * weight
             draws[m] = jnp.where(chan == 0, d_optical * STEP_DEPTH * sg, grad * weight * (sg * (1.0 - sg)))
+        parts, d_raws = [], []
         for s in range(S):
             draw = jnp.where(back, draws[S - 1 - s], draws[s])
             draw = jnp.concatenate([draw[i] for i in range(RC)], 1)
@@ -264,12 +308,13 @@
             high = draw.astype(BF16).astype(F32)
             low = draw - high
             d_raw = jnp.concatenate([high, low, high, jnp.zeros_like(high)], 0).astype(BF16)
-            g_out = blocks(d_raw[:2 * TILE], h2[s, c])
-            du2 = dot(wob_s[...], d_raw) * d2[s, c]
-            both = jnp.concatenate(split(du2), 0)
-            g_mid = blocks(h1[s, c], both)
-            du1 = dot_stacked(wmb_s[...], both) * d1[s, c]
-            g_in = blocks(feats[s, c], jnp.concatenate(split(du1), 0))
+            d_raws.append(d_raw)
+            parts += [backward_part(s, c, j, d_raw) for j in range(n // SUB)]
+        staggered(parts)
+        for s in range(S):
+            g_out = blocks(d_raws[s][:2 * TILE], h2[s, c])
+            g_mid = blocks(h1[s, c], du2s[s])
+            g_in = blocks(feats[s, c], du1s[s])
             grads[0:2] += g_in.reshape(2, TILE, hid)
             grads[2:T - 1] += g_mid.reshape(T - 3, TILE, hid)
             grads[T - 1] += g_out
@@ -342,7 +387,7 @@
             tile_copy(t, 0).wait_send()
             last_copy(t, 1).wait_recv()
 
-    final_out[...] = final[...]
+    final_out[...] = final[...].reshape(final_out.shape)
 
     @pl.when(owns)
     def _():
@@ -351,12 +396,23 @@
             last_copy(my_tile, k).wait_send()
 
 
-def deliver(picture, tiles, image, out_in, out_mid, out_out):
-    T, _, hid = tiles.shape
-    image[...] = picture[...]
-    out_in[...] = tiles[0:2].reshape(2 * TILE, hid)
-    out_mid[...] = tiles[2:T - 1].reshape(hid, hid)
-    out_out[...] = tiles[T - 1][:4]
+def deliver(picture, tiles, image, out_in, out_mid, out_out, sems):
+    fin, hid = out_in.shape[0], out_mid.shape[0]
+    copies = [
+        pltpu.make_async_copy(source, target, sems.at[i])
+        for i, (source, target) in enumerate(
+            (
+                (tiles.at[pl.ds(fin, hid)], out_mid),
+                (picture, image),
+                (tiles.at[pl.ds(0, fin)], out_in),
+                (tiles.at[pl.ds(fin + hid, 4)], out_out),
+            )
+        )
+    ]
+    for copy in copies:
+        copy.start()
+    for copy in copies:
+        copy.wait()
 
 
 def per_device(volume, offsets, shifts, order, cond, w_in, w_mid, w_out, cot_image):
@@ -370,6 +426,7 @@
     n = RC * C
     T = (fin + hid) // TILE + 1
     vmem = pl.BlockSpec(memory_space=pltpu.VMEM)
+    far = pl.BlockSpec(memory_space=pltpu.HBM)
     smem = pl.BlockSpec(memory_space=pltpu.SMEM)
     kept = lambda rows, kind: pltpu.VMEM((S, nch, rows, n), kind)
     dma = lambda *shape: pltpu.SemaphoreType.DMA(shape)
@@ -377,14 +434,21 @@
         functools.partial(kernel, views, bricks, S, R, C, RC, RB, hid),
         out_shape=(
             jax.ShapeDtypeStruct((1, 3, RB, C), F32),
-            jax.ShapeDtypeStruct((T, TILE, hid), F32),
+            jax.ShapeDtypeStruct((T * TILE, hid), F32),
         ),
-        in_specs=[vmem, smem, smem, smem, smem, vmem, vmem, vmem, vmem],
+        in_specs=[far, smem, smem, smem, smem, far, far, far, far],
         out_specs=(vmem, vmem),
         scratch_shapes=[
+            pltpu.VMEM((S, CH * R, C), F32),
+            pltpu.VMEM(w_in.shape, F32),
+            pltpu.VMEM(w_mid.shape, F32),
+            pltpu.VMEM(w_out.shape[::-1], F32),
+            pltpu.VMEM(cot_image.shape, F32),
+            dma(5),
             pltpu.VMEM((CH * R, C), F32),
             pltpu.VMEM((S, 2 * R + 1, CH, C), F32),
             kept(2 * fin, BF16), kept(2 * hid, BF16), kept(hid, F32), kept(2 * hid, BF16), kept(hid, F32),
+            pltpu.VMEM((S, 2 * hid, n), BF16), pltpu.VMEM((S, 2 * hid, n), BF16),
             pltpu.VMEM((S, R, 4, C), F32),
             pltpu.VMEM((S, R, 4, C), F32),
             pltpu.VMEM((bricks, R, 4, C), F32),
@@ -401,7 +465,7 @@
             dma(T), dma(N - 1), dma(N), dma(T),
         ],
         compiler_params=pltpu.CompilerParams(
-            collective_id=0, has_side_effects=True, vmem_limit_bytes=40 * 1024 * 1024
+            collective_id=0, has_side_effects=True, vmem_limit_bytes=60 * 1024 * 1024
         ),
         cost_estimate=pl.CostEstimate(
             flops=2 * S * R * C * hid * (3 * hid + 3 * fin + 12), bytes_accessed=4 * volume.size,
@@ -416,9 +480,10 @@
             jax.ShapeDtypeStruct((hid, hid), F32),
             jax.ShapeDtypeStruct((4, hid), F32),
         ),
-        in_specs=[vmem, vmem],
-        out_specs=(vmem, vmem, vmem, vmem),
-        compiler_params=pltpu.CompilerParams(vmem_limit_bytes=4 * 1024 * 1024),
+        in_specs=[far, far],
+        out_specs=(far, far, far, far),
+        scratch_shapes=[dma(4)],
+        compiler_params=pltpu.CompilerParams(vmem_limit_bytes=60 * 1024 * 1024),
     )(image, tiles)
     return image, g_in, g_mid, g_out.T
 

time: 38.3 us -> 40.4 us (1.055)
  Pallas kernels: 32.8 us -> 39 us
  local copies, waits for them, and re-layouts: 3.86 us -> 0 us
    unnamed x16 -> x0, local copies, waits for them, and re-layouts: 3.86 us -> none
    pallas_call x1, Pallas kernels: 0.65 us -> 3.81 us  [per_device(): pl.pallas_call(deliver, out_shape=(jax.ShapeDtypeStruct((1, 3, RB, C), F3...]
    pallas_call x1, Pallas kernels: 32.2 us -> 35.1 us  [per_device(): pl.pallas_call(functools.partial(kernel, views, bricks, S, R, C, RC, RB,...]
where the time goes in v1:
time: 40.4 us; the launch traced here: 40.2 us
  Pallas kernels  39 us (97%)
  between operations  1.29 us (3%)
    pallas_call x1, Pallas kernels, per_device(): pl.pallas_call(functools.partial(kernel, views, bricks, S, R, C, RC, RB,...  35.1 us
    pallas_call x1, Pallas kernels, per_device(): pl.pallas_call(deliver, out_shape=(jax.ShapeDtypeStruct((1, 3, RB, C), F3...  3.81 us

profile of v1, /device:TPU:0, one launch (start us, length us, event | category | flops | bytes accessed | tf_op | source)
XLA Modules:
  0.0 40.2 jit_solution(13272779577549804665)
XLA Ops:
  1.3 35.1 %shard_map.120 = (f32[1,3,8,128]{3,2,1,0:T(8,128)}, f32[152,128]{1,0:T(8,128)}) custom-call(f32[2,256,128]{2,1,0:T(8,128)} %bitcast.3, f32[1,3]{1,0:T(1,128)} %offsets.1, s32[1,2]{1,0:T(1,128)} %shifts.1, s32[1]{0:T(128)S(6)} %copy.13.order, f32[1,8]{1,0:T(1,128)} %cond.1, f32[16,128]{1,0:T(8,128)} %w_in_far.1, f32[128,128]{1,0:T(8,128)} %w_mid_far.1, ...), custom_call_target="tpu_custom_call" | custom-call | flops 931135488 | bytes 262144 | tf_op jit(solution)/shard_map/pallas_call | solution.py:433
  36.4 3.8 %shard_map.121 = (f32[1,3,8,128]{3,2,1,0:T(8,128)}, f32[16,128]{1,0:T(8,128)}, f32[128,128]{1,0:T(8,128)}, f32[4,128]{1,0:T(4,128)}) custom-call(f32[1,3,8,128]{3,2,1,0:T(8,128)} %get-tuple-element.10.picture, f32[152,128]{1,0:T(8,128)} %get-tuple-element.11.tiles), custom_call_target="tpu_custom_call" | custom-call | tf_op jit(solution)/shard_map/pallas_call | solution.py:475
